TPU v7x, 1024 devices: a whole 4x4x32 slice. The times are simulated.
1024 devices in a mesh: row: 64 (over y, z_lo, core), slab: 16 (over x, z_hi).
Axes of the slice: x: 4, y: 4, z: 32 (z_hi: 4, z_lo: 8; z = z_hi * 8 + z_lo), core: 2. Of those that a mesh axis runs over, the one named last changes fastest.
Arguments:
- features: bfloat16 [256, 262144], P('slab', 'row'), may hold values from -6 to 6
- self_weight: bfloat16 [256, 256], replicated, may hold values from -0.375 to 0.375
- neigh_weight: bfloat16 [256, 256], replicated, may hold values from -0.375 to 0.375
- cotangent: bfloat16 [256, 262144], P(None, ('row', 'slab')), may hold values from -6 to 6
- degree: int32 [262144], P('row'), may hold values from 1 to 1040, as said below
- tile_count: int32 [2048], P('row'), may hold values from 1 to 8, as said below
- tile_cols: int32 [2048, 8], P('row'), may hold values from 0 to 2047
- tile_vals: bfloat16 [2048, 8, 128, 128], P('row'), may hold values from 0 to 1.5, as said below
Outputs:
- output: bfloat16 [256, 262144], P(None, ('row', 'slab'))
- grad_self: float32 [256, 256], P('slab')
- grad_neigh: float32 [256, 256], P('slab')
Inputs may be any that keep to these rules, and one draw needn't show every extreme that they name: `tile_count`: every row of tiles uses between 1 and 8 slots; in every eight consecutive row blocks of 4096 nodes one (drawn) has all 8 slots used in each of its rows of tiles, the others use at most half of the slots. `tile_vals`: nonnegative edge weights, most of them zero. A node's degree is at least one more than the number of nonzero weights in its row of its used tile slots.
All inputs are finite; a program needn't handle non-finite values.
Results may differ from a plain program's by a relative error of at most 0.0029.
Values may be sent and summed in bfloat16 or wider, within the bound.
A program may use at most 64 MiB of HBM per device.

v0:
```python
import math

import jax
import jax.numpy as jnp
from jax import lax
from jax.sharding import PartitionSpec as P


def per_device(
    features, self_weight, neigh_weight, cotangent, degree, tile_count, tile_cols, tile_vals
):
    slab_width = features.shape[0]
    local_rows = features.shape[1]
    tile_len = tile_vals.shape[-1]
    row_tiles = tile_cols.shape[0]
    gathered = lax.all_gather(features, "row", axis=1, tiled=True)
    blocks = gathered.reshape(slab_width, -1, tile_len)
    busiest = jnp.max(tile_count)

    def add_slot(slot_index, totals):
        column_ids = lax.dynamic_index_in_dim(tile_cols, slot_index, 1, keepdims=False)
        picked = jnp.take(blocks, column_ids, axis=1)
        weights = lax.dynamic_index_in_dim(tile_vals, slot_index, 1, keepdims=False)
        partial_sum = jnp.einsum(
            "ftc,tdc->ftd", picked, weights, preferred_element_type=jnp.float32
        )
        active = slot_index < tile_count
        return totals + jnp.where(active[None, :, None], partial_sum, jnp.float32(0.0))

    totals = lax.fori_loop(
        0, busiest, add_slot, jnp.zeros((slab_width, row_tiles, tile_len), jnp.float32)
    )
    mean_agg = (
        totals.reshape(slab_width, local_rows) / degree.astype(jnp.float32)[None, :]
    ).astype(jnp.bfloat16)
    owned_rows, owned_mean = (
        lax.all_to_all(features, "slab", split_axis=1, concat_axis=0, tiled=True),
        lax.all_to_all(mean_agg, "slab", split_axis=1, concat_axis=0, tiled=True),
    )
    projected = jnp.einsum("io,in->on", self_weight, owned_rows, preferred_element_type=jnp.float32)
    projected = projected + jnp.einsum(
        "io,in->on", neigh_weight, owned_mean, preferred_element_type=jnp.float32
    )
    output = projected.astype(jnp.bfloat16)
    factor = 1.0 / math.sqrt(local_rows * lax.axis_size("row"))
    width_out = self_weight.shape[1]
    full_grad = jnp.concatenate(
        [
            jnp.einsum("in,on->io", owned_rows, cotangent, preferred_element_type=jnp.float32),
            jnp.einsum("in,on->io", owned_mean, cotangent, preferred_element_type=jnp.float32),
        ],
        axis=1,
    )
    summed = lax.psum(full_grad, ("row", "slab"))
    slab_grads = lax.dynamic_slice_in_dim(
        summed, lax.axis_index("slab") * slab_width, slab_width, 0
    )
    grad_self = slab_grads[:, :width_out] * factor
    grad_neigh = slab_grads[:, width_out:] * factor
    return (output, grad_self, grad_neigh)


def solution(mesh):
    return jax.shard_map(
        per_device,
        mesh=mesh,
        in_specs=(
            P("slab", "row"),
            P(),
            P(),
            P(None, ("row", "slab")),
            P("row"),
            P("row"),
            P("row", None),
            P("row", None, None, None),
        ),
        out_specs=(P(None, ("row", "slab")), P("slab", None), P("slab", None)),
        check_vma=False,
    )
```

profile of v0, /device:TPU:1, one launch (start us, length us, event | category | flops | bytes accessed | tf_op | source)
XLA Modules:
  0.0 1153.0 jit_solution(2568755949592783340)
XLA Ops:
  7.2 0.7 all-gather.2.cloned.1.call-update
  7.9 1.5 copy.44
  9.5 31.5 %all-to-all-start = ((bf16[16,16,256]{2,0,1:T(8,128)(2,1)}), bf16[16,16,256]{2,0,1:T(8,128)(2,1)S(1)}, u32[]{:S(2)}, u32[]{:S(2)}) async-start(bf16[16,16,256]{2,0,1:T(8,128)(2,1)} %bitcast.39), calls=%async_computation | async-start | bytes 262144 | tf_op jit(solution)/shard_map/all_to_all | solution.py:37
  40.9 0.7 convert_element_type.10
  41.7 1.3 reduce_max.9
  43.0 117.6 %all-gather.2.cloned.1.call-done = bf16[16,262144]{1,0:T(8,128)(2,1)} async-done(((bf16[16,4096]{1,0:T(8,128)(2,1)}), bf16[16,262144]{1,0:T(8,128)(2,1)}) %all-gather.2.cloned.1.call-update) | async-done | bytes 8388624 | tf_op jit(solution)/shard_map/all_gather | solution.py:16
  160.6 7.4 copy_bitcast_fusion
  168.0 29.9 %while.10 = (s32[]{:T(128)}, f32[16,32,128]{2,0,1:T(8,128)S(1)}, s32[]{:T(128)}, s32[32]{0:T(128)S(1)}, bf16[32,8,128,128]{3,2,1,0:T(8,128)(2,1)}, /*index=5*/s3...) while((s32[]{:T(128)}, f32[16,32,128]{2,0,1:T(8,128)S(1)}, s32[]{:T(128)}, ...), condition=%wide.region_2.3_spmd, body=%wide.region_1.2_spmd.sunk | while | flops 16975076 | bytes 1971091 | solution.py:30
  168.8 0.7 and_bitcast_fusion.2
  169.5 4.0 gather_fusion
  173.5 1.9 fusion.27
  176.1 0.7 and_bitcast_fusion.2
  176.8 4.0 gather_fusion
  180.8 1.9 fusion.27
  183.4 0.7 and_bitcast_fusion.2
  184.1 4.0 gather_fusion
  188.1 1.9 fusion.27
  190.7 0.7 and_bitcast_fusion.2
  191.4 4.0 gather_fusion
  195.4 1.9 fusion.27
  198.2 0.7 copy.34
  198.9 20.4 %all-to-all-start.1 = ((bf16[16,16,256]{2,0,1:T(8,128)(2,1)}), bf16[16,16,256]{2,0,1:T(8,128)(2,1)S(1)}, u32[]{:S(2)}, u32[]{:S(2)}) async-start(bf16[16,16,256]{2,0,1:T(8,128)(2,1)} %copy.34), calls=%async_computation.1 | async-start | bytes 262144 | tf_op jit(solution)/shard_map/all_to_all | solution.py:38
  219.3 0.2 fusion.11
  219.5 27.4 %all-to-all-done.1 = bf16[16,16,256]{2,0,1:T(8,128)(2,1)S(1)} async-done(((bf16[16,16,256]{2,0,1:T(8,128)(2,1)}), bf16[16,16,256]{2,0,1:T(8,128)(2,1)S(1)}, u32[]{:S(2)}, u32[]{:S(2)}) %all-to-all-start.1) | async-done | bytes 131104 | tf_op jit(solution)/shard_map/all_to_all | solution.py:38
  246.9 0.2 fusion.12
  247.1 0.8 pad_maximum_fusion
  248.0 0.2 convolution_bitcast_fusion
  248.2 0.9 fusion.10
  249.1 894.6 %all-reduce.2.cloned.1.call-done = f32[256,512]{0,1:T(8,128)} async-done(((f32[256,512]{0,1:T(8,128)}), f32[256,512]{0,1:T(8,128)}) %all-reduce.2.cloned.1.call-update) | async-done | bytes 524304 | tf_op jit(solution)/shard_map/psum | solution.py:54
  1143.7 1.1 dynamic-slice_multiply_fusion
  1144.8 0.7 copy.36
  1145.5 0.7 copy.37
  (25 shorter events, 0.4 us)
Async XLA Ops:
  7.2 212.2 %copy-start = (bf16[256,256]{1,0:T(8,128)(2,1)S(1)}, bf16[256,256]{1,0:T(8,128)(2,1)}, u32[]{:S(2)}) copy-start(bf16[256,256]{1,0:T(8,128)(2,1)} %param.13) | copy-start | bytes 393220
  7.2 153.4 %all-gather.2.cloned.1.call-start = ((), (), s32[]{:S(2)}) async-start(), calls=%async_computation.2 | async-start | bytes 8519680 | tf_op jit(solution)/shard_map/all_gather | solution.py:16
  9.5 189.4 %all-to-all-start = ((bf16[16,16,256]{2,0,1:T(8,128)(2,1)}), bf16[16,16,256]{2,0,1:T(8,128)(2,1)S(1)}, u32[]{:S(2)}, u32[]{:S(2)}) async-start(bf16[16,16,256]{2,0,1:T(8,128)(2,1)} %bitcast.39), calls=%async_computation | async-start | bytes 262144 | tf_op jit(solution)/shard_map/all_to_all | solution.py:37
  42.9 125.1 %copy-start.3 = (s32[32]{0:T(128)S(1)}, s32[32]{0:T(128)}, u32[]{:S(2)}) copy-start(s32[32]{0:T(128)} %param.15) | copy-start | bytes 388
  168.0 80.0 %copy-start.2 = (bf16[256,256]{1,0:T(8,128)(2,1)S(1)}, bf16[256,256]{1,0:T(8,128)(2,1)}, u32[]{:S(2)}) copy-start(bf16[256,256]{1,0:T(8,128)(2,1)} %param.12) | copy-start | bytes 393220
  168.0 80.2 %copy-start.1 = (bf16[256,256]{1,0:T(8,128)(2,1)S(1)}, bf16[256,256]{1,0:T(8,128)(2,1)}, u32[]{:S(2)}) copy-start(bf16[256,256]{1,0:T(8,128)(2,1)} %param.11) | copy-start | bytes 393220
  198.9 48.0 %all-to-all-start.1 = ((bf16[16,16,256]{2,0,1:T(8,128)(2,1)}), bf16[16,16,256]{2,0,1:T(8,128)(2,1)S(1)}, u32[]{:S(2)}, u32[]{:S(2)}) async-start(bf16[16,16,256]{2,0,1:T(8,128)(2,1)} %copy.34), calls=%async_computation.1 | async-start | bytes 262144 | tf_op jit(solution)/shard_map/all_to_all | solution.py:38
  219.3 924.5 %all-reduce.2.cloned.1.call-start = ((), (), s32[]{:S(2)}) async-start(), calls=%async_computation.3 | async-start | bytes 1048576 | tf_op jit(solution)/shard_map/psum | solution.py:54
Sparse Core Ops, SparseCore 0:
  10.8 149.7 all-gather.1
  248.1 895.5 all-reduce.1
where the time goes:
time: 1160 us; the launch traced here: 1150 us
  waiting for transfers between devices  1040 us (90%)
  starting transfers between devices  51.9 us (4%)
  local copies, waits for them, and re-layouts  27.1 us (2%)
  between operations  14.2 us (1%)
    psum x1, waiting for transfers between devices, per_device(): summed = lax.psum(full_grad, ('row', 'slab'))  895 us
    all_gather x1, waiting for transfers between devices, per_device(): gathered = lax.all_gather(features, 'row', axis=1, tiled=True)  118 us
    all_to_all x1, starting transfers between devices, per_device(): lax.all_to_all(features, 'slab', split_axis=1, concat_axis=0, tiled=True)  31.5 us
    all_to_all x1, waiting for transfers between devices, per_device(): lax.all_to_all(mean_agg, 'slab', split_axis=1, concat_axis=0, tiled=True)  27.4 us
  transfers between devices with their start and end apart: 4, of which 3 were waited for; matrix products, arithmetic and copies ran while one was open for 3% of the time, Pallas kernels for 0%

commit v1 on v0

v1 whole, which is shorter than its diff:
```python
import functools
import math

import jax
import jax.numpy as jnp
from jax import lax
from jax.experimental import pallas as pl
from jax.experimental.pallas import tpu as pltpu
from jax.sharding import PartitionSpec as P

NY, NZ, NC = 4, 8, 2
NX, NH = 4, 4
NROW, NSLAB = NY * NZ * NC, NX * NH
WIDTH = 256
TILE = 128
MESH = pl.DeviceIdType.MESH


def nt_dot(a, b):
    return lax.dot_general(a, b, (((1,), (1,)), ((), ())), preferred_element_type=jnp.float32)


def tn_dot(a, b):
    return lax.dot_general(a, b, (((0,), (0,)), ((), ())), preferred_element_type=jnp.float32)


def kernel(
    factor,
    cols_ref,
    feat_ref,
    deg_ref,
    self_ref,
    neigh_ref,
    cot_hbm,
    vals_hbm,
    out_ref,
    gself_ref,
    gneigh_ref,
    buf,
    vals,
    cot,
    mean,
    fown,
    mown,
    oself,
    g,
    r1,
    acc,
    r2,
    acc2,
    r3,
    acc3,
    r4,
    r5,
    r6,
    local_sem,
    zsend,
    ysend,
    hsend,
    csend,
    recv,
    hrecv,
    crecv,
    fsend,
    frecv,
    msend,
    mrecv,
    send1,
    recv1,
    send2,
    recv2,
    send3,
    recv3,
    send4,
    recv4,
    send5,
    recv5,
    send6,
    recv6,
):
    row = lax.axis_index("row")
    slab = lax.axis_index("slab")
    core = lax.rem(row, NC)
    z = lax.rem(lax.div(row, NC), NZ)
    y = lax.div(row, NC * NZ)
    x = lax.div(slab, NH)
    hi = lax.rem(slab, NH)
    per_block = feat_ref.shape[1] // TILE
    half = per_block // 2

    def row_of(yy, zz, cc):
        return (yy * NZ + zz) * NC + cc

    vals_copy = pltpu.make_async_copy(vals_hbm, vals, local_sem.at[0])
    vals_copy.start()
    cot_copy = pltpu.make_async_copy(cot_hbm, cot, local_sem.at[1])
    cot_copy.start()
    for j in range(per_block):
        buf[row * per_block + j] = feat_ref[:, j * TILE : (j + 1) * TILE]
    buf[NROW * per_block] = jnp.zeros((feat_ref.shape[0], TILE), jnp.bfloat16)

    barrier = pltpu.get_barrier_semaphore()
    partners = 0
    for d in range(1, NSLAB):
        pl.semaphore_signal(
            barrier, inc=1, device_id=(row, lax.rem(slab + d, NSLAB)), device_id_type=MESH
        )
        partners += 1
    for d in range(1, NZ):
        pl.semaphore_signal(
            barrier, inc=1, device_id=(row_of(y, lax.rem(z + d, NZ), core), slab), device_id_type=MESH
        )
        partners += 1
    for d in range(NY):
        for e in range(NC):
            if d or e:
                pl.semaphore_signal(
                    barrier,
                    inc=1,
                    device_id=(row_of(lax.rem(y + d, NY), z, lax.rem(core + e, NC)), slab),
                    device_id_type=MESH,
                )
                partners += 1
    pl.semaphore_wait(barrier, partners)

    yup, ydown, yopp = lax.rem(y + 1, NY), lax.rem(y + 3, NY), lax.rem(y + 2, NY)
    mate = row_of(y, z, 1 - core)

    def block(yy, zz, cc):
        return buf.at[pl.ds(row_of(yy, zz, cc) * per_block, per_block)]

    def half_block(yy, zz, which):
        return buf.at[pl.ds(row_of(yy, zz, core) * per_block + which * half, half)]

    def block_copy(yy, zz, send, arrive, target):
        ref = block(yy, zz, core)
        return pltpu.make_async_remote_copy(
            src_ref=ref,
            dst_ref=ref,
            send_sem=send,
            recv_sem=arrive,
            device_id=(target, slab),
            device_id_type=MESH,
        )

    def z_copy(way, zz):
        target = row_of(y, z + (1 - 2 * way), core)
        return block_copy(y, zz, zsend.at[way, zz], recv.at[y, zz], target)

    def y_copy(way, zz):
        target = row_of(ydown if way else yup, z, core)
        return block_copy(y, zz, ysend.at[way, zz], recv.at[y, zz], target)

    def h_copy(way, zz):
        source = yup if way else ydown
        target = row_of(ydown if way else yup, z, core)
        ref = half_block(source, zz, way)
        return pltpu.make_async_remote_copy(
            src_ref=ref,
            dst_ref=ref,
            send_sem=hsend.at[way, zz],
            recv_sem=hrecv.at[way, zz],
            device_id=(target, slab),
            device_id_type=MESH,
        )

    def c_copy(yy, zz):
        return block_copy(yy, zz, csend.at[yy, zz], crecv.at[yy, zz], mate)

    def arrived(yy, zz):
        block_copy(yy, zz, csend.at[yy, zz], recv.at[yy, zz], mate).wait_recv()

    def spread(zz):
        y_copy(0, zz).start()
        y_copy(1, zz).start()
        c_copy(y, zz).start()

    def relay(zz):
        arrived(ydown, zz)
        h_copy(0, zz).start()
        c_copy(ydown, zz).start()
        arrived(yup, zz)
        h_copy(1, zz).start()
        c_copy(yup, zz).start()

    def finish(zz):
        for way in range(2):
            ref = half_block(yopp, zz, way)
            pltpu.make_async_remote_copy(
                src_ref=ref,
                dst_ref=ref,
                send_sem=hsend.at[way, zz],
                recv_sem=hrecv.at[way, zz],
                device_id=(mate, slab),
                device_id_type=MESH,
            ).wait_recv()
        c_copy(yopp, zz).start()

    def f_copy(other):
        return pltpu.make_async_remote_copy(
            src_ref=feat_ref.at[:, pl.ds(pl.multiple_of(other * WIDTH, WIDTH), WIDTH)],
            dst_ref=fown.at[pl.ds(pl.multiple_of(slab * 16, 16), 16), :],
            send_sem=fsend.at[other],
            recv_sem=frecv.at[slab],
            device_id=(row, other),
            device_id_type=MESH,
        )

    def f_wait(other):
        pltpu.make_async_remote_copy(
            src_ref=feat_ref.at[:, pl.ds(0, WIDTH)],
            dst_ref=fown.at[pl.ds(pl.multiple_of(other * 16, 16), 16), :],
            send_sem=fsend.at[other],
            recv_sem=frecv.at[other],
            device_id=(row, other),
            device_id_type=MESH,
        ).wait_recv()

    @pl.when(z < NZ - 1)
    def _():
        z_copy(0, z).start()

    @pl.when(z > 0)
    def _():
        z_copy(1, z).start()

    spread(z)
    LAG, LAG2 = 1, 2

    @pl.loop(1, NZ + LAG2)
    def _(t):
        @pl.when((t < NZ) & (z - t >= 0))
        def _():
            zz = z - t
            arrived(y, zz)

            @pl.when(z < NZ - 1)
            def _():
                z_copy(0, zz).start()

            spread(zz)

        @pl.when((t < NZ) & (z + t < NZ))
        def _():
            zz = z + t
            arrived(y, zz)

            @pl.when(z > 0)
            def _():
                z_copy(1, zz).start()

            spread(zz)

        @pl.when(t == 3)
        def _():
            @pl.loop(1, NSLAB)
            def _(d):
                f_copy(lax.rem(slab + d, NSLAB)).start()

        u = t - LAG

        @pl.when((u < NZ) & (z - u >= 0))
        def _():
            relay(z - u)

        @pl.when((u > 0) & (u < NZ) & (z + u < NZ))
        def _():
            relay(z + u)

        v = t - LAG2

        @pl.when((v >= 0) & (v < NZ) & (z - v >= 0))
        def _():
            finish(z - v)

        @pl.when((v > 0) & (v < NZ) & (z + v < NZ))
        def _():
            finish(z + v)

    @pl.loop(1, NSLAB)
    def _(d):
        f_wait(lax.rem(slab + d, NSLAB))

    fown[pl.ds(pl.multiple_of(slab * 16, 16), 16), :] = feat_ref[
        :, pl.ds(pl.multiple_of(slab * WIDTH, WIDTH), WIDTH)
    ]
    cot_copy.wait()
    oself[...] = tn_dot(self_ref[...], fown[...])

    def keep_grad(q, values):
        for h in range(NC):
            for xx in range(NX):
                for hh in range(NH):
                    for e in range(2):
                        at = (xx * NH + hh) * 16 + e * 8
                        g[h, xx, 2 * q + e, hh] = values[at : at + 8, h * TILE : (h + 1) * TILE]

    keep_grad(0, nt_dot(fown[...], cot[...]))

    vals_copy.wait()

    @pl.loop(0, NY)
    def _(yy):
        @pl.loop(0, NZ)
        def _(zz):
            ref = block(yy, zz, 1 - core)
            pltpu.make_async_remote_copy(
                src_ref=ref,
                dst_ref=ref,
                send_sem=csend.at[yy, zz],
                recv_sem=crecv.at[yy, zz],
                device_id=(mate, slab),
                device_id_type=MESH,
            ).wait_recv()

    def m_copy(other):
        return pltpu.make_async_remote_copy(
            src_ref=mean.at[other],
            dst_ref=mown.at[pl.ds(pl.multiple_of(slab * 16, 16), 16), :],
            send_sem=msend.at[other],
            recv_sem=mrecv.at[slab],
            device_id=(row, other),
            device_id_type=MESH,
        )

    def m_wait(other):
        pltpu.make_async_remote_copy(
            src_ref=mean.at[other],
            dst_ref=mown.at[pl.ds(pl.multiple_of(other * 16, 16), 16), :],
            send_sem=msend.at[other],
            recv_sem=mrecv.at[other],
            device_id=(row, other),
            device_id_type=MESH,
        ).wait_recv()

    slots = cols_ref.shape[1]

    @pl.loop(0, NSLAB)
    def _(d):
        other = lax.rem(slab + 1 + d, NSLAB)
        for p in range(2):
            t = other * 2 + p
            picked = [buf[cols_ref[t, k]] for k in range(slots)]
            weights = jnp.concatenate([vals[t, k] for k in range(slots)], axis=1)
            total = nt_dot(jnp.concatenate(picked, axis=1), weights)
            degree = deg_ref[pl.ds(t, 1), :].astype(jnp.float32)
            mean[other, :, p * TILE : (p + 1) * TILE] = (total / degree).astype(jnp.bfloat16)

        @pl.when(d < NSLAB - 1)
        def _():
            m_copy(other).start()

    mown[pl.ds(pl.multiple_of(slab * 16, 16), 16), :] = mean[slab]

    @pl.loop(1, NSLAB)
    def _(d):
        m_wait(lax.rem(slab + d, NSLAB))

    keep_grad(1, nt_dot(mown[...], cot[...]))

    copy1 = pltpu.make_async_remote_copy(
        src_ref=g.at[1 - core],
        dst_ref=r1,
        send_sem=send1,
        recv_sem=recv1,
        device_id=(mate, slab),
        device_id_type=MESH,
    )
    copy1.start()
    out_ref[...] = (oself[...] + tn_dot(neigh_ref[...], mown[...])).astype(jnp.bfloat16)
    copy1.wait_recv()
    acc[...] = g[core] + r1[...]

    def stage(src, dst, sends, recvs, size, me, target):
        copies = []
        for d in range(1, size):
            other = lax.rem(me + d, size)
            copies.append(
                pltpu.make_async_remote_copy(
                    src_ref=src(other),
                    dst_ref=dst.at[me],
                    send_sem=sends.at[other],
                    recv_sem=recvs.at[me],
                    device_id=target(other),
                    device_id_type=MESH,
                )
            )
        for c in copies:
            c.start()
        return copies

    def take(src, dst, sends, recvs, size, me, target):
        for d in range(1, size):
            other = lax.rem(me + d, size)
            pltpu.make_async_remote_copy(
                src_ref=src(other),
                dst_ref=dst.at[other],
                send_sem=sends.at[other],
                recv_sem=recvs.at[other],
                device_id=target(other),
                device_id_type=MESH,
            ).wait_recv()

    def exchange(*a):
        copies = stage(*a)
        take(*a)
        return copies

    started = []
    started += exchange(
        lambda o: acc.at[o], r2, send2, recv2, NX, x, lambda o: (row, o * NH + hi)
    )
    total = acc[x]
    for d in range(1, NX):
        total = total + r2[lax.rem(x + d, NX)]
    acc2[...] = total
    started += exchange(
        lambda o: acc2.at[o], r3, send3, recv3, NY, y, lambda o: (row_of(o, z, core), slab)
    )
    total = acc2[y]
    for d in range(1, NY):
        total = total + r3[lax.rem(y + d, NY)]
    acc3[...] = total
    started += exchange(
        lambda o: acc3.at[o], r4, send4, recv4, NH, hi, lambda o: (row, x * NH + o)
    )
    total = acc3[hi]
    for d in range(1, NH):
        total = total + r4[lax.rem(hi + d, NH)]
    r5[z] = total
    started += exchange(
        lambda o: r5.at[z], r5, send5, recv5, NZ, z, lambda o: (row_of(y, o, core), slab)
    )
    total = r5[0]
    for i in range(1, NZ):
        total = total + r5[i]
    spot = y * NC + core
    r6[spot] = total * factor
    started += exchange(
        lambda o: r6.at[spot],
        r6,
        send6,
        recv6,
        NY * NC,
        spot,
        lambda o: (row_of(lax.div(o, NC), z, lax.rem(o, NC)), slab),
    )
    for q, ref in enumerate((gself_ref, gneigh_ref)):
        for e in range(2):
            for c in range(NC):
                ref[e * 8 : (e + 1) * 8, c * TILE : (c + 1) * TILE] = r6[(2 * q + e) * NC + c]

    for c in started:
        c.wait_send()
    copy1.wait_send()

    @pl.loop(1, NSLAB)
    def _(d):
        f_copy(lax.rem(slab + d, NSLAB)).wait_send()
        m_copy(lax.rem(slab + d, NSLAB)).wait_send()

    @pl.loop(0, NZ)
    def _(zz):
        @pl.when((z < NZ - 1) & (zz <= z))
        def _():
            z_copy(0, zz).wait_send()

        @pl.when((z > 0) & (zz >= z))
        def _():
            z_copy(1, zz).wait_send()

        for way in range(2):
            y_copy(way, zz).wait_send()
            h_copy(way, zz).wait_send()

        @pl.loop(0, NY)
        def _(yy):
            c_copy(yy, zz).wait_send()


def per_device(
    features, self_weight, neigh_weight, cotangent, degree, tile_count, tile_cols, tile_vals
):
    width, nodes = features.shape
    tiles, slots = tile_cols.shape
    factor = 1.0 / math.sqrt(nodes * NROW)
    f32, bf16 = jnp.float32, jnp.bfloat16
    dma = pltpu.SemaphoreType.DMA
    vmem = pl.BlockSpec(memory_space=pltpu.VMEM)
    smem = pl.BlockSpec(memory_space=pltpu.SMEM)
    hbm = pl.BlockSpec(memory_space=pl.ANY)
    return pl.pallas_call(
        functools.partial(kernel, factor),
        out_shape=(
            jax.ShapeDtypeStruct((WIDTH, WIDTH), bf16),
            jax.ShapeDtypeStruct((width, WIDTH), f32),
            jax.ShapeDtypeStruct((width, WIDTH), f32),
        ),
        in_specs=[smem, vmem, vmem, vmem, vmem, hbm, hbm],
        out_specs=(vmem, vmem, vmem),
        scratch_shapes=[
            pltpu.VMEM((NROW * tiles + 1, width, TILE), bf16),
            pltpu.VMEM(tile_vals.shape, bf16),
            pltpu.VMEM((WIDTH, WIDTH), bf16),
            pltpu.VMEM((NSLAB, width, WIDTH), bf16),
            pltpu.VMEM((WIDTH, WIDTH), bf16),
            pltpu.VMEM((WIDTH, WIDTH), bf16),
            pltpu.VMEM((WIDTH, WIDTH), f32),
            pltpu.VMEM((NC, NX, NY, NH, 8, TILE), f32),
            pltpu.VMEM((NX, NY, NH, 8, TILE), f32),
            pltpu.VMEM((NX, NY, NH, 8, TILE), f32),
            pltpu.VMEM((NX, NY, NH, 8, TILE), f32),
            pltpu.VMEM((NY, NH, 8, TILE), f32),
            pltpu.VMEM((NY, NH, 8, TILE), f32),
            pltpu.VMEM((NH, 8, TILE), f32),
            pltpu.VMEM((NH, 8, TILE), f32),
            pltpu.VMEM((NZ, 8, TILE), f32),
            pltpu.VMEM((NY * NC, 8, TILE), f32),
            dma((2,)),
            dma((2, NZ)),
            dma((2, NZ)),
            dma((2, NZ)),
            dma((NY, NZ)),
            dma((NY, NZ)),
            dma((2, NZ)),
            dma((NY, NZ)),
            dma((NSLAB,)),
            dma((NSLAB,)),
            dma((NSLAB,)),
            dma((NSLAB,)),
            dma(()),
            dma(()),
            dma((NX,)),
            dma((NX,)),
            dma((NY,)),
            dma((NY,)),
            dma((NH,)),
            dma((NH,)),
            dma((NZ,)),
            dma((NZ,)),
            dma((NY * NC,)),
            dma((NY * NC,)),
        ],
        compiler_params=pltpu.CompilerParams(
            collective_id=0, has_side_effects=True, vmem_limit_bytes=40 * 1024 * 1024
        ),
    )(
        jnp.where(jnp.arange(slots)[None, :] < tile_count[:, None], tile_cols, NROW * tiles),
        features,
        degree.reshape(tiles, TILE),
        self_weight,
        neigh_weight,
        cotangent,
        tile_vals,
    )


def solution(mesh):
    return jax.shard_map(
        per_device,
        mesh=mesh,
        in_specs=(
            P("slab", "row"),
            P(),
            P(),
            P(None, ("row", "slab")),
            P("row"),
            P("row"),
            P("row", None),
            P("row", None, None, None),
        ),
        out_specs=(P(None, ("row", "slab")), P("slab", None), P("slab", None)),
        check_vma=False,
    )
```

time: 1160 us -> 146 us (0.13)
  waiting for transfers between devices: 1040 us -> 0 us
  Pallas kernels: 0 us -> 134 us
  starting transfers between devices: 51.9 us -> 0 us
  local copies, waits for them, and re-layouts: 27.1 us -> 10.3 us
  between operations: 14.2 us -> 0.65 us
    psum x1 -> x0, waiting for transfers between devices: 895 us -> none  [per_device(): summed = lax.psum(full_grad, ('row', 'slab'))]
    pallas_call x0 -> x1, Pallas kernels: none -> 134 us  [per_device(): pl.pallas_call(functools.partial(kernel, factor), out_shape=(jax.ShapeDty...]
    all_gather x1 -> x0, waiting for transfers between devices: 118 us -> none  [per_device(): gathered = lax.all_gather(features, 'row', axis=1, tiled=True)]
    all_to_all x2 -> x0, starting transfers between devices: 51.8 us -> none  [the longest x1 31.5 us: per_device(): lax.all_to_all(features, 'slab', split_axis=1, concat_axis=0, tiled=True)]
    all_to_all x2 -> x0, waiting for transfers between devices: 27.4 us -> none  [the longest x1 27.4 us: per_device(): lax.all_to_all(mean_agg, 'slab', split_axis=1, concat_axis=0, tiled=True)]
    gather x4 -> x0, local copies, waits for them, and re-layouts: 15.9 us -> none  [add_slot(): picked = jnp.take(blocks, column_ids, axis=1)]
  transfers between devices with their start and end apart: 4 -> 0, of which waited for: 3 -> 0; matrix products, arithmetic and copies ran while one was open for 3% -> 0% of each run, Pallas kernels for 0% -> 0%
where the time goes in v1:
time: 146 us
  Pallas kernels  134 us (92%)
  local copies, waits for them, and re-layouts  10.3 us (7%)
    pallas_call x1, Pallas kernels, per_device(): pl.pallas_call(functools.partial(kernel, factor), out_shape=(jax.ShapeDty...  134 us
    unnamed x16, local copies, waits for them, and re-layouts  10.3 us

profile of v1, /device:TPU:1, one launch (start us, length us, event | category | flops | bytes accessed | tf_op | source)
XLA Modules:
  0.0 145.5 jit_solution(12779467119760386802)
XLA Ops:
  0.6 0.8 copy.11
  1.4 0.7 fusion.cols_ref
  2.1 0.0 copy-start
  2.1 3.4 %copy-done = bf16[32,8,128,128]{3,2,1,0:T(8,128)(2,1)S(1)} copy-done((bf16[32,8,128,128]{3,2,1,0:T(8,128)(2,1)S(1)}, bf16[32,8,128,128]{3,2,1,0:T(8,128)(2,1)}, u32[]{:S(2)}) %copy-start) | copy-done | bytes 8388632
  5.5 0.0 copy-start.1
  5.5 0.9 copy-done.1
  6.4 0.0 copy-start.2
  6.4 0.9 copy-done.2
  7.3 0.0 copy-start.3
  7.3 0.9 copy-done.3
  8.2 0.0 copy-start.4
  8.2 0.9 copy-done.4
  9.1 0.0 copy-start.5
  9.1 0.7 copy-done.5
  9.8 133.8 %shard_map.103 = (bf16[256,256]{1,0:T(8,128)(2,1)S(1)}, f32[16,256]{1,0:T(8,128)S(1)}, f32[16,256]{1,0:T(8,128)S(1)}) custom-call(s32[32,8]{1,0:T(8,128)S(1)} %fusion.cols_ref, bf16[16,4096]{1,0:T(8,128)(2,1)S(1)} %copy-done.1, s32[32,128]{1,0:T(8,128)S(1)} %bitcast.1, bf16[256,256]{1,0:T(8,128)(2,1)S(1)} %copy-done.2, bf16[256,256]{1,0:T(8,128)(2,1)S(1)} %copy-done.3, ...), custom_call_target="tpu_custom_call" | custom-call | tf_op jit(solution)/shard_map/pallas_call | solution.py:492
  143.6 0.7 copy.15
  144.3 0.6 copy.16
  144.9 0.6 copy.17
Async XLA Ops:
  2.1 3.4 %copy-start = (bf16[32,8,128,128]{3,2,1,0:T(8,128)(2,1)S(1)}, bf16[32,8,128,128]{3,2,1,0:T(8,128)(2,1)}, u32[]{:S(2)}) copy-start(bf16[32,8,128,128]{3,2,1,0:T(8,128)(2,1)} %vals_hbm.1) | copy-start | bytes 25165828
  5.5 0.9 copy-start.1
  6.4 0.9 copy-start.2
  7.3 0.9 copy-start.3
  8.2 0.9 copy-start.4
  9.1 0.7 copy-start.5

commit v2 on v0

v2 whole, which is shorter than its diff:
```python
import functools
import math

import jax
import jax.numpy as jnp
from jax import lax
from jax.experimental import pallas as pl
from jax.experimental.pallas import tpu as pltpu
from jax.sharding import PartitionSpec as P

NY, NZ, NC = 4, 8, 2
NX, NH = 4, 4
NROW, NSLAB = NY * NZ * NC, NX * NH
WIDTH = 256
TILE = 128
PART = 16
ROUNDS = (1, 2, 4, 8, 1)
MESH = pl.DeviceIdType.MESH


def nt_dot(a, b):
    return lax.dot_general(a, b, (((1,), (1,)), ((), ())), preferred_element_type=jnp.float32)


def tn_dot(a, b):
    return lax.dot_general(a, b, (((0,), (0,)), ((), ())), preferred_element_type=jnp.float32)


def wrap(value, size):
    return jnp.where(value >= size, value - size, value)


def kernel(
    factor,
    index_ref,
    feat_hbm,
    vals_hbm,
    cot_hbm,
    self_hbm,
    neigh_hbm,
    deg_hbm,
    out_ref,
    gself_ref,
    gneigh_ref,
    feat,
    vals,
    self_ref,
    neigh_ref,
    deg_ref,
    buf,
    cot,
    fown,
    mean,
    mown,
    oself,
    g,
    ra,
    acc,
    rb,
    acc2,
    rh,
    rz,
    rd,
    told,
    local_sem,
    zsend,
    ysend,
    hsend,
    csend,
    recv,
    hrecv,
    crecv,
    fsend,
    frecv,
    msend,
    mrecv,
    asend,
    arecv,
    bsend,
    brecv,
    hisend,
    hirecv,
    zlsend,
    zlrecv,
    dsend,
    drecv,
):
    row = lax.axis_index("row")
    slab = lax.axis_index("slab")
    core = lax.rem(row, NC)
    z = lax.rem(lax.div(row, NC), NZ)
    y = lax.div(row, NC * NZ)
    x = lax.div(slab, NH)
    hi = lax.rem(slab, NH)
    mate = row + 1 - 2 * core
    per_block = feat.shape[1] // TILE
    half = per_block // 2

    def row_of(yy, zz, cc):
        return (yy * NZ + zz) * NC + cc

    def start_of(yy, zz, cc):
        return ((cc * NY + yy) * NZ + zz) * per_block

    def remote(src, dst, send, arrive, device):
        return pltpu.make_async_remote_copy(
            src_ref=src,
            dst_ref=dst,
            send_sem=send,
            recv_sem=arrive,
            device_id=device,
            device_id_type=MESH,
        )

    barrier = pltpu.get_barrier_semaphore()
    def along(d):
        at = lax.rem(hi * NZ + z + d + NH * NZ, NH * NZ)
        return (row_of(y, lax.rem(at, NZ), core), x * NH + lax.div(at, NZ))

    partners = [along(1), along(-1), (mate, slab)]
    partners += [
        (r, wrap(x + d, NX) * NH + hi) for d in range(1, NX) for r in (row, mate)
    ]
    partners += [
        (row_of(wrap(y + d, NY), z, c), slab) for d in range(1, NY) for c in range(NC)
    ]
    for partner in partners:
        pl.semaphore_signal(barrier, inc=1, device_id=partner, device_id_type=MESH)
    loads = [
        pltpu.make_async_copy(src, dst, local_sem.at[i])
        for i, (src, dst) in enumerate(
            (
                (feat_hbm, feat),
                (cot_hbm, cot),
                (vals_hbm, vals),
                (self_hbm, self_ref),
                (neigh_hbm, neigh_ref),
                (deg_hbm, deg_ref),
            )
        )
    ]
    for load in loads:
        load.start()
    loads[0].wait()
    own = start_of(y, z, core)
    for j in range(per_block):
        buf[own + j] = feat[:, j * TILE : (j + 1) * TILE]
    buf[NROW * per_block] = jnp.zeros((PART, TILE), jnp.bfloat16)
    pl.semaphore_wait(barrier, len(partners))

    def tell(k):
        for side, step in enumerate((ROUNDS[k], -ROUNDS[k])):
            pl.semaphore_signal(
                told.at[k, side], inc=1, device_id=along(step), device_id_type=MESH
            )

    def hear(k):
        for side in range(2):
            pl.semaphore_wait(told.at[k, side], 1)

    tell(0)
    yup, ydown, yopp = wrap(y + 1, NY), wrap(y + 3, NY), wrap(y + 2, NY)

    def block(yy, zz, cc):
        return buf.at[pl.ds(start_of(yy, zz, cc), per_block)]

    def half_block(yy, zz, which):
        return buf.at[pl.ds(start_of(yy, zz, core) + which * half, half)]

    def z_copy(way, zz):
        ref = block(y, zz, core)
        target = row_of(y, z + 1 - 2 * way, core)
        return remote(ref, ref, zsend.at[way, zz], recv.at[y, zz], (target, slab))

    def z_out(way, zz):
        @pl.when((z > 0) if way else (z < NZ - 1))
        def _():
            z_copy(way, zz).start()

    def y_copy(way, zz):
        ref = block(y, zz, core)
        target = row_of(ydown if way else yup, z, core)
        return remote(ref, ref, ysend.at[way, zz], recv.at[y, zz], (target, slab))

    def h_copy(way, zz):
        ref = half_block(yup if way else ydown, zz, way)
        target = row_of(ydown if way else yup, z, core)
        return remote(ref, ref, hsend.at[way, zz], hrecv.at[way, zz], (target, slab))

    def c_copy(yy, zz):
        ref = block(yy, zz, core)
        return remote(ref, ref, csend.at[yy, zz], crecv.at[yy, zz], (mate, slab))

    def arrived(yy, zz):
        ref = block(yy, zz, core)
        remote(ref, ref, csend.at[yy, zz], recv.at[yy, zz], (mate, slab)).wait_recv()

    def spread(zz):
        y_copy(0, zz).start()
        y_copy(1, zz).start()
        c_copy(y, zz).start()

    def relay(zz):
        arrived(ydown, zz)
        h_copy(0, zz).start()
        c_copy(ydown, zz).start()
        arrived(yup, zz)
        h_copy(1, zz).start()
        c_copy(yup, zz).start()

    def finish(zz):
        for way in range(2):
            ref = half_block(yopp, zz, way)
            remote(ref, ref, hsend.at[way, zz], hrecv.at[way, zz], (mate, slab)).wait_recv()
        c_copy(yopp, zz).start()

    def f_copy(other):
        src = feat.at[:, pl.ds(pl.multiple_of(other * WIDTH, WIDTH), WIDTH)]
        dst = fown.at[pl.ds(pl.multiple_of(slab * PART, PART), PART), :]
        return remote(src, dst, fsend.at[other], frecv.at[slab], (row, other))

    z_out(0, z)
    z_out(1, z)
    spread(z)
    LAG, LAG2 = 1, 2

    @pl.loop(1, NZ + LAG2)
    def _(t):
        @pl.when((t < NZ) & (z - t >= 0))
        def _():
            arrived(y, z - t)
            z_out(0, z - t)
            spread(z - t)

        @pl.when((t < NZ) & (z + t < NZ))
        def _():
            arrived(y, z + t)
            z_out(1, z + t)
            spread(z + t)

        for k, when in enumerate((1, 2, 3, 4, 5)):

            @pl.when(t == when)
            def _():
                hear(k)
                if k + 1 < len(ROUNDS):
                    tell(k + 1)
                else:

                    @pl.loop(1, NSLAB)
                    def _(d):
                        f_copy(wrap(slab + d, NSLAB)).start()

        u = t - LAG

        @pl.when((u < NZ) & (z - u >= 0))
        def _():
            relay(z - u)

        @pl.when((u > 0) & (u < NZ) & (z + u < NZ))
        def _():
            relay(z + u)

        v = t - LAG2

        @pl.when((v >= 0) & (v < NZ) & (z - v >= 0))
        def _():
            finish(z - v)

        @pl.when((v > 0) & (v < NZ) & (z + v < NZ))
        def _():
            finish(z + v)

    a_peers = [
        (wrap(core + e, NC), wrap(x + d, NX)) for d in range(NX) for e in range(NC) if d or e
    ]
    y_peers = [wrap(y + d, NY) for d in range(1, NY)]
    h_peers = [wrap(hi + d, NH) for d in range(1, NH)]
    z_peers = [wrap(z + d, NZ) for d in range(1, NZ)]
    d_peers = [(yy, c) for yy in y_peers for c in range(NC)] + [(y, 1 - core)]

    def a_copy(q, peer, arriving=False):
        cc, xx = peer
        mine = (cc, xx) if arriving else (core, x)
        device = (row_of(y, z, cc), xx * NH + hi)
        return remote(
            g.at[q, cc, xx],
            ra.at[q, mine[0], mine[1]],
            asend.at[q, cc, xx],
            arecv.at[q, mine[0], mine[1]],
            device,
        )

    def b_copy(yy, arriving=False):
        mine = yy if arriving else y
        device = (row_of(yy, z, core), slab)
        return remote(acc.at[yy], rb.at[mine], bsend.at[yy], brecv.at[mine], device)

    def hi_copy(hh, arriving=False):
        mine = hh if arriving else hi
        device = (row, x * NH + hh)
        return remote(acc2.at[hh], rh.at[mine], hisend.at[hh], hirecv.at[mine], device)

    def zl_copy(zz, arriving=False):
        mine = zz if arriving else z
        device = (row_of(y, zz, core), slab)
        return remote(rz.at[z], rz.at[mine], zlsend.at[zz], zlrecv.at[mine], device)

    def d_copy(peer, arriving=False):
        yy, c = peer
        mine = (yy, c) if arriving else (y, core)
        device = (row_of(yy, z, c), slab)
        return remote(
            rd.at[y, core],
            rd.at[mine[0], mine[1]],
            dsend.at[yy, c],
            drecv.at[mine[0], mine[1]],
            device,
        )

    def begin_sum(q, left):
        total = nt_dot(left, cot[...])
        for c in range(NC):
            for xx in range(NX):
                for hh in range(NH):
                    for e in range(2):
                        at = (xx * NH + hh) * PART + e * 8
                        g[q, c, xx, e, hh] = total[at : at + 8, c * TILE : (c + 1) * TILE]
        for peer in a_peers:
            a_copy(q, peer).start()

    def after_a(q):
        total = g[q, core, x]
        for peer in a_peers:
            a_copy(q, peer, True).wait_recv()
            total = total + ra[q, peer[0], peer[1]]
        acc[2 * q : 2 * q + 2] = total

    @pl.loop(0, NY)
    def _(yy):
        @pl.loop(0, NZ)
        def _(zz):
            ref = block(yy, zz, 1 - core)
            remote(
                ref, ref, csend.at[yy, zz], crecv.at[yy, zz], (mate, slab)
            ).wait_recv()

    loads[2].wait()
    loads[5].wait()

    def m_copy(other):
        dst = mown.at[pl.ds(pl.multiple_of(slab * PART, PART), PART), :]
        return remote(mean.at[other], dst, msend.at[other], mrecv.at[slab], (row, other))

    slots = index_ref.shape[0]

    @pl.loop(0, NH)
    def _(dh):
        hh = wrap(wrap(hi + 2, NH) + dh, NH)

        @pl.loop(0, NX)
        def _(dx):
            other = wrap(x + 1 + dx, NX) * NH + hh
            for p in range(2):
                t = other * 2 + p
                picked = [buf[index_ref[k, t]] for k in range(slots)]
                weights = jnp.concatenate([vals[t, k] for k in range(slots)], axis=1)
                total = nt_dot(jnp.concatenate(picked, axis=1), weights)
                degree = deg_ref[pl.ds(t, 1), :].astype(jnp.float32)
                mean[other, :, p * TILE : (p + 1) * TILE] = (total / degree).astype(jnp.bfloat16)

            @pl.when(other != slab)
            def _():
                m_copy(other).start()

    mown[pl.ds(pl.multiple_of(slab * PART, PART), PART), :] = mean[slab]

    fown[pl.ds(pl.multiple_of(slab * PART, PART), PART), :] = feat[
        :, pl.ds(pl.multiple_of(slab * WIDTH, WIDTH), WIDTH)
    ]
    loads[1].wait()

    @pl.loop(1, NSLAB)
    def _(d):
        other = wrap(slab + d, NSLAB)
        dst = fown.at[pl.ds(pl.multiple_of(other * PART, PART), PART), :]
        src = feat.at[:, pl.ds(0, WIDTH)]
        remote(src, dst, fsend.at[other], frecv.at[other], (row, other)).wait_recv()

    begin_sum(0, fown[...])
    loads[3].wait()
    loads[4].wait()
    oself[...] = tn_dot(self_ref[...], fown[...])

    @pl.loop(1, NSLAB)
    def _(d):
        f_copy(wrap(slab + d, NSLAB)).wait_send()

    @pl.loop(0, NZ)
    def _(zz):
        @pl.when((z < NZ - 1) & (zz <= z))
        def _():
            z_copy(0, zz).wait_send()

        @pl.when((z > 0) & (zz >= z))
        def _():
            z_copy(1, zz).wait_send()

        for way in range(2):
            y_copy(way, zz).wait_send()
            h_copy(way, zz).wait_send()

        @pl.loop(0, NY)
        def _(yy):
            c_copy(yy, zz).wait_send()

    after_a(0)
    for peer in a_peers:
        a_copy(0, peer).wait_send()

    @pl.loop(1, NSLAB)
    def _(d):
        other = wrap(slab + d, NSLAB)
        dst = mown.at[pl.ds(pl.multiple_of(other * PART, PART), PART), :]
        remote(mean.at[other], dst, msend.at[other], mrecv.at[other], (row, other)).wait_recv()

    begin_sum(1, mown[...])
    after_a(1)
    for yy in y_peers:
        b_copy(yy).start()
    total = acc[y]
    for yy in y_peers:
        b_copy(yy, True).wait_recv()
        total = total + rb[yy]
    acc2[...] = total
    for hh in h_peers:
        hi_copy(hh).start()
    out_ref[...] = (oself[...] + tn_dot(neigh_ref[...], mown[...])).astype(jnp.bfloat16)
    for peer in a_peers:
        a_copy(1, peer).wait_send()
    for yy in y_peers:
        b_copy(yy).wait_send()

    @pl.loop(1, NSLAB)
    def _(d):
        m_copy(wrap(slab + d, NSLAB)).wait_send()

    total = acc2[hi]
    for hh in h_peers:
        hi_copy(hh, True).wait_recv()
        total = total + rh[hh]
    rz[z] = total
    for zz in z_peers:
        zl_copy(zz).start()
    for hh in h_peers:
        hi_copy(hh).wait_send()
    for zz in z_peers:
        zl_copy(zz, True).wait_recv()
    total = rz[0]
    for i in range(1, NZ):
        total = total + rz[i]
    rd[y, core] = total * factor
    for peer in d_peers:
        d_copy(peer).start()
    for zz in z_peers:
        zl_copy(zz).wait_send()
    for peer in d_peers:
        d_copy(peer, True).wait_recv()
    for q, ref in enumerate((gself_ref, gneigh_ref)):
        for e in range(2):
            for c in range(NC):
                ref[e * 8 : (e + 1) * 8, c * TILE : (c + 1) * TILE] = rd[2 * q + e, c]
    for peer in d_peers:
        d_copy(peer).wait_send()


def per_device(
    features, self_weight, neigh_weight, cotangent, degree, tile_count, tile_cols, tile_vals
):
    width, nodes = features.shape
    tiles, slots = tile_cols.shape
    factor = 1.0 / math.sqrt(nodes * NROW)
    owner = tile_cols // tiles
    place = (owner % NC * (NROW // NC) + owner // NC) * tiles + tile_cols % tiles
    used = jnp.arange(slots)[None, :] < tile_count[:, None]
    index = jnp.where(used, place, NROW * tiles).T
    f32, bf16 = jnp.float32, jnp.bfloat16
    vmem = pltpu.VMEM
    dma = pltpu.SemaphoreType.DMA
    in_vmem = pl.BlockSpec(memory_space=pltpu.VMEM)
    return pl.pallas_call(
        functools.partial(kernel, factor),
        out_shape=(
            jax.ShapeDtypeStruct((WIDTH, WIDTH), bf16),
            jax.ShapeDtypeStruct((width, WIDTH), f32),
            jax.ShapeDtypeStruct((width, WIDTH), f32),
        ),
        in_specs=[pl.BlockSpec(memory_space=pltpu.SMEM)] + [pl.BlockSpec(memory_space=pl.ANY)] * 6,
        out_specs=(in_vmem, in_vmem, in_vmem),
        scratch_shapes=[
            vmem((width, nodes), bf16),
            vmem(tile_vals.shape, bf16),
            vmem((WIDTH, WIDTH), bf16),
            vmem((WIDTH, WIDTH), bf16),
            vmem((tiles, TILE), jnp.int32),
            vmem((NROW * tiles + 1, width, TILE), bf16),
            vmem((WIDTH, WIDTH), bf16),
            vmem((WIDTH, WIDTH), bf16),
            vmem((NSLAB, width, WIDTH), bf16),
            vmem((WIDTH, WIDTH), bf16),
            vmem((WIDTH, WIDTH), f32),
            vmem((2, NC, NX, 2, NH, 8, TILE), f32),
            vmem((2, NC, NX, 2, NH, 8, TILE), f32),
            vmem((NY, NH, 8, TILE), f32),
            vmem((NY, NH, 8, TILE), f32),
            vmem((NH, 8, TILE), f32),
            vmem((NH, 8, TILE), f32),
            vmem((NZ, 8, TILE), f32),
            vmem((NY, NC, 8, TILE), f32),
            pltpu.SemaphoreType.REGULAR((len(ROUNDS), 2)),
            dma((6,)),
            dma((2, NZ)),
            dma((2, NZ)),
            dma((2, NZ)),
            dma((NY, NZ)),
            dma((NY, NZ)),
            dma((2, NZ)),
            dma((NY, NZ)),
            dma((NSLAB,)),
            dma((NSLAB,)),
            dma((NSLAB,)),
            dma((NSLAB,)),
            dma((2, NC, NX)),
            dma((2, NC, NX)),
            dma((NY,)),
            dma((NY,)),
            dma((NH,)),
            dma((NH,)),
            dma((NZ,)),
            dma((NZ,)),
            dma((NY, NC)),
            dma((NY, NC)),
        ],
        compiler_params=pltpu.CompilerParams(
            collective_id=0, has_side_effects=True, vmem_limit_bytes=60 * 1024 * 1024
        ),
    )(
        index,
        features,
        tile_vals,
        cotangent,
        self_weight,
        neigh_weight,
        degree.reshape(tiles, TILE),
    )


def solution(mesh):
    return jax.shard_map(
        per_device,
        mesh=mesh,
        in_specs=(
            P("slab", "row"),
            P(),
            P(),
            P(None, ("row", "slab")),
            P("row"),
            P("row"),
            P("row", None),
            P("row", None, None, None),
        ),
        out_specs=(P(None, ("row", "slab")), P("slab", None), P("slab", None)),
        check_vma=False,
    )
```

time: 1160 us -> 133 us (0.11)
  waiting for transfers between devices: 1040 us -> 0 us
  Pallas kernels: 0 us -> 126 us
  starting transfers between devices: 51.9 us -> 0 us
  local copies, waits for them, and re-layouts: 27.1 us -> 4.21 us
  between operations: 14.2 us -> 0.64 us
    psum x1 -> x0, waiting for transfers between devices: 895 us -> none  [per_device(): summed = lax.psum(full_grad, ('row', 'slab'))]
    pallas_call x0 -> x1, Pallas kernels: none -> 126 us  [per_device(): pl.pallas_call(functools.partial(kernel, factor), out_shape=(jax.ShapeDty...]
    all_gather x1 -> x0, waiting for transfers between devices: 118 us -> none  [per_device(): gathered = lax.all_gather(features, 'row', axis=1, tiled=True)]
    all_to_all x2 -> x0, starting transfers between devices: 51.8 us -> none  [the longest x1 31.5 us: per_device(): lax.all_to_all(features, 'slab', split_axis=1, concat_axis=0, tiled=True)]
    all_to_all x2 -> x0, waiting for transfers between devices: 27.4 us -> none  [the longest x1 27.4 us: per_device(): lax.all_to_all(mean_agg, 'slab', split_axis=1, concat_axis=0, tiled=True)]
    gather x4 -> x0, local copies, waits for them, and re-layouts: 15.9 us -> none  [add_slot(): picked = jnp.take(blocks, column_ids, axis=1)]
  transfers between devices with their start and end apart: 4 -> 0, of which waited for: 3 -> 0; matrix products, arithmetic and copies ran while one was open for 3% -> 0% of each run, Pallas kernels for 0% -> 0%
where the time goes in v2:
time: 133 us; the launch traced here: 132 us
  Pallas kernels  126 us (95%)
  local copies, waits for them, and re-layouts  4.21 us (3%)
    pallas_call x1, Pallas kernels, per_device(): pl.pallas_call(functools.partial(kernel, factor), out_shape=(jax.ShapeDty...  126 us
    unnamed x3, local copies, waits for them, and re-layouts  4.21 us

profile of v2, /device:TPU:1, one launch (start us, length us, event | category | flops | bytes accessed | tf_op | source)
XLA Modules:
  0.0 132.1 jit_solution(14659206051795908626)
XLA Ops:
  0.6 1.3 fusion.5.index_ref
  1.9 126.0 %shard_map.103 = (bf16[256,256]{1,0:T(8,128)(2,1)}, f32[16,256]{1,0:T(8,128)}, f32[16,256]{1,0:T(8,128)}) custom-call(s32[8,32]{1,0:T(8,128)} %fusion.5.index_ref, bf16[16,4096]{1,0:T(8,128)(2,1)} %feat_hbm.1, bf16[32,8,128,128]{3,2,1,0:T(8,128)(2,1)} %vals_hbm.1, bf16[256,256]{1,0:T(8,128)(2,1)} %cot_hbm.1, bf16[256,256]{1,0:T(8,128)(2,1)} %self_hbm.1, ...), custom_call_target="tpu_custom_call" | custom-call | tf_op jit(solution)/shard_map/pallas_call | solution.py:491
  127.9 1.6 %copy.14 = bf16[256,256]{1,0:T(8,128)(2,1)} copy(bf16[256,256]{1,0:T(8,128)(2,1)} %get-tuple-element.6) | data formatting | bytes 262144
  129.5 1.3 %copy.15 = f32[16,256]{1,0:T(8,128)} copy(f32[16,256]{1,0:T(8,128)} %get-tuple-element.7) | data formatting | bytes 32768
  130.8 1.3 %copy.16 = f32[16,256]{1,0:T(8,128)} copy(f32[16,256]{1,0:T(8,128)} %get-tuple-element.8) | data formatting | bytes 32768
